TPU v7x, 32 devices: a whole 2x2x4 slice. The times are simulated.
32 devices in a mesh: dp: 4 (over z), expert: 8 (over y, x, core).
Axes of the slice: x: 2, y: 2, z: 4, core: 2. Of those that a mesh axis runs over, the one named last changes fastest.
Arguments:
- tokens: bfloat16 [16384, 768], P(('dp', 'expert')), may hold values from -6 to 6
- segment_ids: int32 [32, 512], P(('dp', 'expert')), may hold values from 0 to 3, never falling along the last dimension, each value on 1 to 256 neighbouring positions
- token_expert: int32 [16384, 1], P(('dp', 'expert')), may hold values from 0 to 7; in each aligned block of 512 rows (0 to 511, 512 to 1023, ...) at most 128 rows name the same one
- gates: float32 [16384], P(('dp', 'expert')), may hold values from 0.3 to 1
- ln1_gain: float32 [768], replicated, may hold values from 0.1 to 1.9
- w_qkv: bfloat16 [768, 2304], replicated, may hold values from -0.21875 to 0.21875
- w_out: bfloat16 [768, 768], replicated, may hold values from -1.25 to 1.25
- ln2_gain: float32 [768], replicated, may hold values from 0.1 to 1.9
- expert_in: bfloat16 [8, 768, 3072], P('expert'), may hold values from -0.21875 to 0.21875
- expert_out: bfloat16 [8, 3072, 768], P('expert'), may hold values from -0.109375 to 0.109375
- cotangent: bfloat16 [16384, 768], P(('dp', 'expert')), may hold values from -6 to 6
Outputs:
- block_out: bfloat16 [16384, 768], P(('dp', 'expert'))
- grad_tokens: bfloat16 [16384, 768], P(('dp', 'expert'))
- grad_ln1: float32 [768], P('dp')
- grad_qkv: float32 [768, 2304], P(None, 'dp')
- grad_out: float32 [768, 768], P(None, 'dp')
- grad_ln2: float32 [768], P('dp')
- grad_expert_in: float32 [8, 768, 3072], P('expert', 'dp')
- grad_expert_out: float32 [8, 3072, 768], P('expert', 'dp')
Inputs may be any that keep to these rules, and one draw needn't show every extreme that they name: `token_expert`: in the 512 rows of one device no expert is named by more than 128 tokens; in some device one expert is named exactly 128 times. `segment_ids`: within a row the numbers never fall; each document has 1 to 256 positions, one exactly that many.
All inputs are finite; a program needn't handle non-finite values.
Results may differ from a plain program's by a relative error of at most 0.012.
Values may be sent and summed in bfloat16 or wider, within the bound.
A program may use at most 192 MiB of HBM per device.

v0:
```python
import functools

import jax
import jax.numpy as jnp
from jax import lax
from jax.experimental import pallas as pl
from jax.experimental.pallas import tpu as pltpu
from jax.sharding import PartitionSpec as P

HEAD_DIM = 64
EPSILON = 1e-05
NEG_LARGE = -1e30
BAND = 128
PAIR = 2 * HEAD_DIM
GROUP = 256
CHUNK = 512
MIB = 2**20
MESH = pl.DeviceIdType.MESH
ANY = pl.BlockSpec(memory_space=pl.ANY)
VMEM = pl.BlockSpec(memory_space=pltpu.VMEM)
f32, bf16 = jnp.float32, jnp.bfloat16


def dot(a, b):
    return jnp.dot(a, b, preferred_element_type=f32)


def dot_nt(a, b):
    return lax.dot_general(a, b, (((1,), (1,)), ((), ())), preferred_element_type=f32)


def dot_tn(a, b):
    return lax.dot_general(a, b, (((0,), (0,)), ((), ())), preferred_element_type=f32)


def flip(index, bits):
    place = 1
    while bits:
        if bits % 2:
            index = index + place * (1 - 2 * ((index // place) % 2))
        bits, place = bits // 2, place * 2
    return index


def add(a, b):
    return (a.astype(f32) + b.astype(f32)).astype(bf16)


def rows_at(start, size):
    return pl.ds(pl.multiple_of(start, size), size)


def greet(peers):
    barrier = pltpu.get_barrier_semaphore()
    for peer in peers:
        pl.semaphore_signal(barrier, inc=1, device_id=peer, device_id_type=MESH)
    pl.semaphore_wait(barrier, len(peers))


def sides(dp):
    side = dp // 2
    return flip(dp, 1), 3 - dp, [3 * (1 - side), 2 - side, 3 * side, 1 + side]


class Relay:
    def __init__(self, dp, me, moves, ssem, rsem):
        self.outer = (dp == 0) | (dp == 3)
        self.inner = jnp.logical_not(self.outer)
        beside, across, _ = sides(dp)
        self.moves = []
        for i, (kind, source, target) in enumerate(moves):
            plane = across if kind == "across" else beside
            copy = pltpu.make_async_remote_copy(
                src_ref=source, dst_ref=target, send_sem=ssem.at[i], recv_sem=rsem.at[i],
                device_id=(plane, me), device_id_type=MESH,
            )
            sender = self.outer if kind == "inward" else self.inner
            receiver = self.outer if kind == "outward" else self.inner
            self.moves.append((copy, sender, receiver))

    def start(self, *which):
        for i in which:
            copy, sender, _ = self.moves[i]
            pl.when(sender)(copy.start)

    def sent(self, i):
        pl.when(self.moves[i][1])(self.moves[i][0].wait_send)

    def landed(self, i):
        pl.when(self.moves[i][2])(self.moves[i][0].wait_recv)

    def merged(self, first, second, total, spare, sem):
        @pl.when(self.inner)
        def _():
            loads = [
                pltpu.make_async_copy(first, total, sem.at[0]),
                pltpu.make_async_copy(second, spare, sem.at[1]),
            ]
            for one in loads:
                one.start()
            for one in loads:
                one.wait()
            lines = total.shape[0] // 12

            @pl.loop(0, 12)
            def _(r):
                at = rows_at(r * lines, lines)
                total[at] = add(total[at], spare[at])


def band(index):
    first = max(0, index - 2) * BAND
    return first, (index + 1) * BAND - first


def column_of(row):
    size = row.shape[1]
    eye = lax.broadcasted_iota(jnp.int32, (size, size), 0) == lax.broadcasted_iota(
        jnp.int32, (size, size), 1
    )
    return jnp.sum(jnp.where(eye, row, 0.0), axis=1, keepdims=True)


def slot_row(experts, num_experts, capacity):
    rows = experts.shape[1]
    lines = max(16, num_experts)
    onehot = lax.broadcasted_iota(jnp.int32, (lines, rows), 0) == experts
    onehot = jnp.where(onehot, 1.0, 0.0)
    before = lax.broadcasted_iota(jnp.int32, (rows, rows), 0) < lax.broadcasted_iota(
        jnp.int32, (rows, rows), 1
    )
    earlier = dot(onehot.astype(bf16), jnp.where(before, 1.0, 0.0).astype(bf16))
    rank = jnp.sum(onehot * earlier, axis=0, keepdims=True)
    return experts.astype(f32) * float(capacity) + rank


def centred(hidden):
    centre = hidden - jnp.mean(hidden, axis=-1, keepdims=True)
    spread = jnp.mean(centre * centre, axis=-1, keepdims=True)
    return centre, lax.rsqrt(spread + EPSILON)


def gelu_pair(x):
    bell = jnp.exp(-0.5 * x * x)
    t = 1.0 / (1.0 + (0.3275911 * 0.7071067811865476) * jnp.abs(x))
    poly = 0.5 * 1.061405429
    for factor in (-1.453152027, 1.421413741, -0.284496736, 0.254829592):
        poly = poly * t + 0.5 * factor
    tail = poly * t * bell
    phi = jnp.where(x >= 0.0, 1.0 - tail, tail)
    return x * phi, phi + x * (bell * 0.3989422804014327)


def gelu(x):
    return gelu_pair(x)[0]


def forward_kernel(groups, cap, ends, *refs):
    (
        tok_hbm, seg_ref, te_ref, gate_ref, g1_ref, wqkv_hbm, wout_hbm, g2_ref, win_hbm, wdown_hbm,
        cot_hbm, h1_out, qkv_out, att_out, inv_out, probs_out, act_out, gpre_out,
    ) = refs[:18]
    count = 4 if ends else 1
    ups, downs = refs[18 : 18 + count], refs[18 + count : 18 + 2 * count]
    up_land = refs[18 + 2 * count : 18 + 2 * count + ends]
    (
        tok, cot, win, wdown, low, h1, place, sent, gy_send, gy_got, v_got, gy_low, spot_own, gy_line,
        v_line, spot_far, gy_fsend, far_send, gy_far, v_far, act,
        gpre, load, store, act_store, gpre_store, gy_ssem, gy_rsem, v_ssem, v_rsem, gy_fssem,
        gy_frsem, v_fssem, v_frsem, line_ssem, line_rsem, rel_s, rel_r,
    ) = refs[18 + 2 * count + ends :]
    dp, me = lax.axis_index("dp"), lax.axis_index("expert")
    rows, width = tok.shape
    slots, hidden = act.shape
    pairs = width // PAIR
    outer = (dp == 0) | (dp == 3)
    inner = jnp.logical_not(outer)
    first_loads = [
        pltpu.make_async_copy(src, dst, load.at[i])
        for i, (src, dst) in enumerate(
            ((cot_hbm, cot), (tok_hbm, tok), (win_hbm, win), (wdown_hbm, wdown))
        )
    ]
    first_loads[0].start()
    first_loads[1].start()
    beside = [(flip(dp, 1), me)] if ends else []
    greet([(dp, flip(me, k)) for k in range(1, groups)] + beside)

    def exchange(source, target, send, receive, k):
        peer = flip(me, k)
        return pltpu.make_async_remote_copy(
            src_ref=source.at[rows_at(peer * cap, cap)],
            dst_ref=target.at[rows_at(me * cap, cap)],
            send_sem=send.at[k],
            recv_sem=receive.at[k],
            device_id=(dp, peer),
            device_id_type=MESH,
        )

    gy_copies = [exchange(gy_send, gy_got, gy_ssem, gy_rsem, k) for k in range(1, groups)]
    v_copies = [exchange(sent, v_got, v_ssem, v_rsem, k) for k in range(1, groups)]
    far_groups = groups if ends else 0
    gy_fars = [exchange(gy_fsend, gy_far, gy_fssem, gy_frsem, k) for k in range(1, far_groups)]
    v_fars = [exchange(far_send, v_far, v_fssem, v_frsem, k) for k in range(1, far_groups)]
    lines = ends and [
        pltpu.make_async_remote_copy(
            src_ref=source, dst_ref=target, send_sem=line_ssem.at[i], recv_sem=line_rsem.at[i],
            device_id=(flip(dp, 1), me), device_id_type=MESH,
        )
        for i, (source, target) in enumerate(
            ((spot_own, spot_far), (gy_low, gy_line), (low, v_line))
        )
    ]

    def when(condition, action):
        if ends:
            pl.when(condition)(action)

    def placed(line, target):
        @pl.loop(0, slots // GROUP)
        def _(g):
            at = rows_at(g * GROUP, GROUP)
            here = lax.broadcasted_iota(jnp.int32, (GROUP, rows), 0) + g * GROUP
            there = jnp.where(here.astype(f32) == spot_far[0:1], 1.0, 0.0).astype(bf16)
            target[at] = dot(there, line[...]).astype(bf16)

    def far_gy():
        lines[0].wait_recv()
        lines[1].wait_recv()
        placed(gy_line, gy_fsend)
        for one in gy_fars:
            one.start()
        gy_far[mine] = gy_fsend[mine]

    def far_v():
        lines[2].wait_recv()
        placed(v_line, far_send)
        for one in v_fars:
            one.start()
        v_far[mine] = far_send[mine]

    mine = rows_at(me * cap, cap)

    def attention(wqkv, wout, qkv, att, inv, probs, bias):
        loads = [
            pltpu.make_async_copy(wqkv_hbm, wqkv, load.at[4]),
            pltpu.make_async_copy(wout_hbm, wout, load.at[5]),
        ]
        for one in loads + first_loads[2:]:
            one.start()
        spot = slot_row(te_ref[...], groups, cap)

        @pl.loop(0, slots // GROUP)
        def _(g):
            here = lax.broadcasted_iota(jnp.int32, (GROUP, rows), 0) + g * GROUP
            there = jnp.where(here.astype(f32) == spot, 1.0, 0.0)
            place[rows_at(g * GROUP, GROUP)] = there.astype(bf16)

        first_loads[0].wait()
        gate = column_of(gate_ref[...])
        gy_low[...] = (gate * cot[...].astype(f32)).astype(bf16)
        if ends:
            spot_own[...] = jnp.broadcast_to(spot, spot_own.shape)

            @pl.when(outer)
            def _():
                lines[0].start()
                lines[1].start()

        @pl.loop(0, slots // GROUP)
        def _(g):
            at = rows_at(g * GROUP, GROUP)
            gy_send[at] = dot(place[at], gy_low[...]).astype(bf16)

        for one in gy_copies:
            one.start()
        gy_got[mine] = gy_send[mine]
        segs = seg_ref[...].astype(f32)
        seg_col = column_of(segs)
        for i in range(rows // BAND):
            first, wide = band(i)
            causal = (lax.broadcasted_iota(jnp.int32, (BAND, wide), 0) + i * BAND) >= (
                lax.broadcasted_iota(jnp.int32, (BAND, wide), 1) + first
            )
            same = seg_col[i * BAND : (i + 1) * BAND] == segs[:, first : first + wide]
            bias[i * BAND : (i + 1) * BAND, 0:wide] = jnp.where(causal & same, 0.0, NEG_LARGE)

        first_loads[1].wait()

        @pl.loop(0, rows // BAND)
        def _(r):
            at = rows_at(r * BAND, BAND)
            centre, inverse = centred(tok[at].astype(f32))
            low[at] = (centre * inverse * g1_ref[...].reshape(1, width)).astype(bf16)

        loads[0].wait()

        @pl.loop(0, 3 * width // GROUP)
        def _(c):
            at = rows_at(c * GROUP, GROUP)
            qkv[:, at] = dot(low[...], wqkv[:, at]).astype(bf16)

        left = lax.broadcasted_iota(jnp.int32, (1, PAIR), 1) < HEAD_DIM
        none, unit = jnp.zeros((), bf16), jnp.ones((), bf16)

        def attend(h):
            at = rows_at(h * PAIR, PAIR)
            k_at = rows_at(width + h * PAIR, PAIR)
            v_at = rows_at(2 * width + h * PAIR, PAIR)
            for i in range(rows // BAND):
                first, wide = band(i)
                here = slice(i * BAND, (i + 1) * BAND)
                keys = qkv[first : first + wide, k_at]
                values = qkv[first : first + wide, v_at]
                query = qkv[here, at] * jnp.asarray(HEAD_DIM**-0.5, bf16)
                query = jnp.concatenate(
                    [jnp.where(left, query, none), jnp.where(left, none, query)], axis=0
                )
                scores = dot_nt(query, keys).reshape(2, BAND, wide) + bias[here, 0:wide][None]
                weights = jnp.exp(scores - jnp.max(scores, axis=-1, keepdims=True)).astype(bf16)
                probs[h, 2 * i * BAND : 2 * (i + 1) * BAND, 0:wide] = weights.reshape(
                    2 * BAND, wide
                )
                one = dot(weights[0], jnp.where(left, values, unit))
                two = dot(weights[1], jnp.where(left, unit, values))
                scale = 1.0 / pltpu.roll(jnp.where(left, two, one), HEAD_DIM, 1)
                inv[here, at] = scale
                att[here, at] = (jnp.where(left, one, two) * scale).astype(bf16)

        pl.loop(0, pairs)(attend)
        when(inner, far_gy)
        stores = [
            pltpu.make_async_copy(src, dst, store.at[i])
            for i, (src, dst) in enumerate(
                ((qkv, qkv_out), (probs, probs_out), (att, att_out), (inv, inv_out))
            )
        ]
        for one in stores:
            one.start()
        loads[1].wait()

        @pl.loop(0, rows // BAND)
        def _(r):
            at = rows_at(r * BAND, BAND)
            resid = tok[at].astype(f32) + dot(att[at], wout[...])
            h1[at] = resid
            centre, inverse = centred(resid)
            low[at] = (centre * inverse * g2_ref[...].reshape(1, width)).astype(bf16)

        when(outer, lambda: lines[2].start())

        @pl.loop(0, slots // GROUP)
        def _(g):
            at = rows_at(g * GROUP, GROUP)
            sent[at] = dot(place[at], low[...]).astype(bf16)

        for one in v_copies:
            one.start()
        v_got[mine] = sent[mine]
        for one in stores:
            one.wait()

    pl.run_scoped(
        attention,
        pltpu.VMEM((width, 3 * width), bf16), pltpu.VMEM((width, width), bf16),
        pltpu.VMEM((rows, 3 * width), bf16), pltpu.VMEM((rows, width), bf16),
        pltpu.VMEM((rows, width), f32), pltpu.VMEM((pairs, 2 * rows, 3 * BAND), bf16),
        pltpu.VMEM((rows, 3 * BAND), f32),
    )

    def experts(act_far, gdown, gup, turned):
        stores = [pltpu.make_async_copy(h1, h1_out, store.at[4])]
        stores[0].start()
        for one in first_loads[2:]:
            one.wait()
        for one in gy_copies:
            one.wait_recv()

        @pl.loop(0, hidden // GROUP)
        def _(c):
            at = rows_at(c * GROUP, GROUP)
            gpre[:, at] = dot_nt(gy_got[...], wdown[at]).astype(bf16)

        many = GROUP // cap
        for g in range(slots // GROUP):
            for k in range(g * many, (g + 1) * many):
                if k:
                    v_copies[k - 1].wait_recv()
            at = rows_at(flip(me // many, g) * GROUP, GROUP)

            @pl.loop(0, hidden // CHUNK)
            def _(c):
                cols = rows_at(c * CHUNK, CHUNK)
                value, back = gelu_pair(dot(v_got[at], win[:, cols]))
                act[at, cols] = value.astype(bf16)
                gpre[at, cols] = (gpre[at, cols].astype(f32) * back).astype(bf16)

            for source, target, sem in ((act, act_out, act_store), (gpre, gpre_out, gpre_store)):
                stores.append(pltpu.make_async_copy(source.at[at], target.at[at], sem.at[g]))
                stores[-1].start()
            if g == 1:
                when(inner, far_v)

        turned[...] = v_got[...].T

        @pl.loop(0, hidden // GROUP)
        def _(c):
            cols = rows_at(c * GROUP, GROUP)
            gup[:, cols] = dot(turned[...], gpre[:, cols]).astype(bf16)

        shares = sides(dp)[2] if ends else [0]
        size, share = width // count, hidden // count
        for i, (one, part) in enumerate(zip(shares, ups)):
            source = gup.at[rows_at(one * size, size)]
            stores.append(pltpu.make_async_copy(source, part, store.at[5 + i]))
            stores[-1].start()
        if ends:
            relay = Relay(
                dp, me, [("inward", gup.at[rows_at(shares[0] * size, size)], up_land[0])],
                rel_s, rel_r,
            )
            relay.start(0)

        def down(kept, shared):
            for i in kept:

                @pl.loop(0, share // GROUP)
                def _(c):
                    cols = pl.ds(pl.multiple_of(shares[i] * share + c * GROUP, GROUP), GROUP)
                    at = pl.ds(pl.multiple_of(i * share + c * GROUP, GROUP), GROUP)
                    total = dot_tn(act[:, cols], gy_got[...])
                    if shared:
                        total = total + dot_tn(act_far[:, at], gy_far[...])
                    gdown[at] = total.astype(bf16)

            for i in kept:
                at = slice(i * share, (i + 1) * share)
                pltpu.make_async_copy(gdown.at[at], downs[i], store.at[9 + i]).start()

        def taken(kept):
            for i in kept:
                at = slice(i * share, (i + 1) * share)
                pltpu.make_async_copy(gdown.at[at], downs[i], store.at[9 + i]).wait()

        def inside():
            for g in range(slots // GROUP):
                for k in range(g * many, (g + 1) * many):
                    if k:
                        v_fars[k - 1].wait_recv()
                at = rows_at(flip(me // many, g) * GROUP, GROUP)
                for i in range(2):

                    @pl.loop(0, share // CHUNK + share % CHUNK // GROUP)
                    def _(c):
                        wide = share // (share // CHUNK + share % CHUNK // GROUP)
                        cols = pl.ds(pl.multiple_of(shares[i] * share + c * wide, 128), wide)
                        kept = pl.ds(pl.multiple_of(i * share + c * wide, 128), wide)
                        act_far[at, kept] = gelu(dot(v_far[at], win[:, cols])).astype(bf16)

            for one in gy_fars:
                one.wait_recv()
            down([0, 1], True)
            for one in gy_fars + v_fars:
                one.wait_send()
            taken([0, 1])

        down([2, 3] if ends else [0], False)
        if ends:
            pl.when(inner)(inside)

            @pl.when(outer)
            def _():
                for one in lines:
                    one.wait_send()

        taken([2, 3] if ends else [0])
        for one in gy_copies + v_copies:
            one.wait_send()
        for one in stores:
            one.wait()
        if ends:
            relay.landed(0)
            relay.sent(0)

    pl.run_scoped(
        experts,
        pltpu.VMEM((slots, hidden // 2) if ends else (16, 128), bf16),
        pltpu.VMEM((hidden, width), bf16), pltpu.VMEM((width, hidden), bf16),
        pltpu.VMEM((width, slots), bf16),
    )


def forward(groups, cap, ends, tokens, segs, experts, gates, g1, w_qkv, w_out, g2, w_in, w_down, cot):
    rows, width = tokens.shape
    hidden = w_in.shape[1]
    slots = groups * cap
    pairs = width // PAIR
    wide = 3 * BAND
    count = 4 if ends else 1
    parts = [(width // count, hidden)] * count + [(hidden // count, width)] * count
    parts += [(width // count, hidden)] * ends
    shapes = [
        ((rows, width), f32), ((rows, 3 * width), bf16), ((rows, width), bf16), ((rows, width), f32),
        ((pairs, 2 * rows, wide), bf16), ((slots, hidden), bf16), ((slots, hidden), bf16),
    ] + [(one, bf16) for one in parts]
    sems = pltpu.SemaphoreType.DMA
    lines = pltpu.VMEM((rows, width), bf16)
    block = pltpu.VMEM((slots, width), bf16)
    tiny = (16, 128)
    far = block if ends else pltpu.VMEM(tiny, bf16)
    far_line = lines if ends else pltpu.VMEM(tiny, bf16)
    return pl.pallas_call(
        functools.partial(forward_kernel, groups, cap, int(ends)),
        out_shape=[jax.ShapeDtypeStruct(*one) for one in shapes],
        in_specs=[ANY, VMEM, VMEM, VMEM, VMEM, ANY, ANY, VMEM, ANY, ANY, ANY],
        out_specs=[ANY] * len(shapes),
        scratch_shapes=[
            lines, lines, pltpu.VMEM(w_in.shape, bf16), pltpu.VMEM(w_down.shape, bf16), lines,
            pltpu.VMEM((rows, width), f32), pltpu.VMEM((slots, rows), bf16), block, block, block,
            block, lines, pltpu.VMEM((8, rows), f32), far_line, far_line, pltpu.VMEM((8, rows), f32),
            far, far, far, far,
            pltpu.VMEM((slots, hidden), bf16), pltpu.VMEM((slots, hidden), bf16),
            sems((6,)), sems((13,)), sems((slots // GROUP,)), sems((slots // GROUP,)),
        ]
        + [sems((groups,))] * 8
        + [sems((3,))] * 2
        + [sems((1,))] * 2,
        compiler_params=pltpu.CompilerParams(
            collective_id=0, has_side_effects=True, vmem_limit_bytes=60 * MIB
        ),
        cost_estimate=pl.CostEstimate(
            flops=200 * 10**9, bytes_accessed=40 * 10**6, transcendentals=10**7
        ),
        name="forward",
    )(tokens, segs, experts, gates, g1, w_qkv, w_out, g2, w_in, w_down, cot)


def backward_kernel(groups, cap, copies, ends, *refs):
    (
        act_hbm, gpre_hbm, win_hbm, wdown_hbm, te_ref, gate_ref, h1_hbm, cot_hbm, tok_hbm, g1_ref,
        g2_ref, att_hbm, inv_hbm, probs_hbm, qkv_hbm, wqkv_hbm, wout_hbm,
    ) = refs[:17]
    parts, refs = refs[17 : 17 + 9 * ends], refs[17 + 9 * ends :]
    block_out, gtok_out, whole_out, total_ref = refs[:4]
    landed, refs = refs[4 : 4 + 9 * ends], refs[4 + 9 * ends :]
    (
        gv_send, gvr, y_send, yr, dense, other, got, ring, ring_got, final, whole, gains_ref,
        gains_pair, gains_chip, gains_part, gains_ring, load, store, gv_ssem, gv_rsem, y_ssem, y_rsem,
        s_pair, r_pair, s_chip, r_chip, s_ring, r_ring, s_out, r_out, s_gain, r_gain, rel_s, rel_r,
        pool_sem, *pools,
    ) = refs
    dp, me = lax.axis_index("dp"), lax.axis_index("expert")
    slots, width = gvr.shape
    rows, hidden = tok_hbm.shape[0], win_hbm.shape[1]
    rounds = [lax.rem(dp + k, copies) for k in range(copies)]
    half = groups // 2
    per, wide = got.shape[1:]
    many = GROUP // cap
    mine = rows_at(me * cap, cap)

    def exchange(source, target, ssem, rsem):
        return [
            pltpu.make_async_remote_copy(
                src_ref=source.at[rows_at(flip(me, k) * cap, cap)],
                dst_ref=target.at[rows_at(me * cap, cap)],
                send_sem=ssem.at[k],
                recv_sem=rsem.at[k],
                device_id=(dp, flip(me, k)),
                device_id_type=MESH,
            )
            for k in range(1, groups)
        ]

    gv_copies = exchange(gv_send, gvr, gv_ssem, gv_rsem)
    y_copies = exchange(y_send, yr, y_ssem, y_rsem)
    relay = None
    if ends:
        up_far, up_near, up_out, up_own, up_far_in, down_far, down_near, down_out, down_own = parts
        relay = Relay(
            dp, me,
            [
                ("inward", up_near, landed[0]), ("inward", down_own, landed[1]),
                ("inward", up_own, landed[2]), ("across", down_far, landed[3]),
                ("across", pools[0], landed[4]), ("across", pools[1], landed[5]),
                ("across", down_near, landed[6]), ("outward", pools[2], landed[7]),
                ("outward", pools[3], landed[8]),
            ],
            rel_s, rel_r,
        )

    def first():
        if ends:
            relay.start(0, 3)
            relay.merged(up_far, up_far_in, pools[0], pools[4], pool_sem)
            relay.start(4)

    def second():
        if ends:
            relay.sent(0)
            relay.start(1)
            relay.landed(0)
            relay.merged(up_near, landed[0], pools[1], pools[4], pool_sem)
            relay.start(5)

    def third():
        if ends:
            relay.sent(1)
            relay.start(2, 6)
            relay.landed(3)
            relay.merged(down_out, landed[3], pools[2], pools[5], pool_sem)
            relay.landed(4)
            relay.merged(up_out, landed[4], pools[3], pools[4], pool_sem)
            relay.start(7, 8)

    def experts(act, gpre, win, wdown):
        loads = [
            pltpu.make_async_copy(src, dst, load.at[i])
            for i, (src, dst) in enumerate(
                ((win_hbm, win), (gpre_hbm, gpre), (wdown_hbm, wdown), (act_hbm, act))
            )
        ]
        for one in loads:
            one.start()
        greet(
            [(dp, flip(me, k)) for k in range(1, groups)] + [(one, me) for one in rounds[1:]]
        )
        first()
        for one in loads[:2]:
            one.wait()
        for g in range(slots // GROUP - 1, -1, -1):
            at = rows_at(flip(me // many, g) * GROUP, GROUP)

            @pl.loop(0, width // GROUP)
            def _(n):
                cols = rows_at(n * GROUP, GROUP)
                gv_send[at, cols] = dot_nt(gpre[at], win[cols]).astype(bf16)

            for k in range(g * many, (g + 1) * many):
                if k:
                    gv_copies[k - 1].start()
        gvr[mine] = gv_send[mine]
        for one in loads[2:]:
            one.wait()

        @pl.loop(0, width // GROUP)
        def _(n):
            cols = rows_at(n * GROUP, GROUP)
            y_send[:, cols] = dot(act[...], wdown[:, cols]).astype(bf16)

    pl.run_scoped(
        experts,
        pltpu.VMEM((slots, hidden), bf16), pltpu.VMEM((slots, hidden), bf16),
        pltpu.VMEM((width, hidden), bf16), pltpu.VMEM((hidden, width), bf16),
    )

    def dense_part(
        h1, cot, tok, att, inv, probs, qkv, wqkv, wout, place, gh1, low, gatt, inner_sum, gqkv,
        turned, gk, gvv, outv,
    ):
        loads = [
            pltpu.make_async_copy(src, dst, load.at[i])
            for i, (src, dst) in enumerate(
                (
                    (h1_hbm, h1), (cot_hbm, cot), (att_hbm, att), (wout_hbm, wout), (inv_hbm, inv),
                    (qkv_hbm, qkv), (probs_hbm, probs), (tok_hbm, tok), (wqkv_hbm, wqkv),
                )
            )
        ]
        for one in loads:
            one.start()
        spot = column_of(slot_row(te_ref[...], groups, cap))
        for r in range(rows // BAND):
            at = slice(r * BAND, (r + 1) * BAND)
            here = lax.broadcasted_iota(jnp.int32, (BAND, slots), 1).astype(f32)
            place[at] = jnp.where(here == spot[at], 1.0, 0.0).astype(bf16)
        gate = column_of(gate_ref[...])
        gains_ref[...] = jnp.zeros_like(gains_ref)
        for one in gv_copies:
            one.wait_recv()
        for one in y_copies:
            one.start()
        yr[mine] = y_send[mine]
        second()
        for i in range(2):
            loads[i].wait()
        for r in range(rows // BAND):
            at = slice(r * BAND, (r + 1) * BAND)
            back = dot(place[at], gvr[...])
            resid = h1[at]
            centre, inverse = centred(resid)
            unit = centre * inverse
            gains_ref[1:2] += jnp.sum(back * unit, axis=0, keepdims=True)
            slant = back * g2_ref[...].reshape(1, width)
            inner = slant - jnp.mean(slant, axis=-1, keepdims=True)
            inner = inner - unit * jnp.mean(slant * unit, axis=-1, keepdims=True)
            grad = cot[at].astype(f32) + inverse * inner
            gh1[at] = grad
            low[at] = grad.astype(bf16)
        for i in range(2, 5):
            loads[i].wait()

        @pl.loop(0, width // GROUP)
        def _(n):
            cols = rows_at(n * GROUP, GROUP)
            grad = dot_nt(low[...], wout[cols]) * inv[:, cols]
            gatt[:, cols] = grad.astype(bf16)
            inner_sum[:, cols] = grad * att[:, cols].astype(f32) * HEAD_DIM**-0.5

        turned[...] = att[...].T

        @pl.loop(0, width // GROUP)
        def _(n):
            cols = rows_at(n * GROUP, GROUP)
            dense[0:width, rows_at(3 * width + n * GROUP, GROUP)] = dot(
                turned[...], low[:, cols]
            ).astype(bf16)

        loads[5].wait()
        loads[6].wait()
        left = lax.broadcasted_iota(jnp.int32, (1, PAIR), 1) < HEAD_DIM
        none = jnp.zeros((), bf16)

        def halves(block):
            return jnp.concatenate([jnp.where(left, block, none), jnp.where(left, none, block)], axis=0)

        @pl.loop(0, width // PAIR)
        def _(h):
            at = rows_at(h * PAIR, PAIR)
            k_at = rows_at(width + h * PAIR, PAIR)
            v_at = rows_at(2 * width + h * PAIR, PAIR)
            gk[...] = jnp.zeros_like(gk)
            gvv[...] = jnp.zeros_like(gvv)
            for i in range(rows // BAND):
                first, wide = band(i)
                mine, seen = slice(i * BAND, (i + 1) * BAND), slice(first, first + wide)
                keys = qkv[seen, k_at]
                values = qkv[seen, v_at] * jnp.asarray(HEAD_DIM**-0.5, bf16)
                query, grad = halves(qkv[mine, at]), halves(gatt[mine, at])
                share = probs[h, 2 * i * BAND : 2 * (i + 1) * BAND, 0:wide]
                inner = inner_sum[mine, at]
                middle = jnp.concatenate(
                    [
                        jnp.sum(jnp.where(left, inner, 0.0), axis=-1, keepdims=True),
                        jnp.sum(jnp.where(left, 0.0, inner), axis=-1, keepdims=True),
                    ],
                    axis=0,
                )
                graw = (share.astype(f32) * (dot_nt(grad, values) - middle)).astype(bf16)
                gquery = dot(graw, keys)
                gqkv[mine, at] = jnp.where(left, gquery[0:BAND], gquery[BAND:]).astype(bf16)
                gk[seen] += dot_tn(graw, query)
                gvv[seen] += dot_tn(share, grad)
            gqkv[:, k_at] = gk[...].astype(bf16)
            gqkv[:, v_at] = gvv[...].astype(bf16)
        loads[7].wait()
        loads[8].wait()
        for r in range(rows // BAND):
            at = slice(r * BAND, (r + 1) * BAND)
            centre, inverse = centred(tok[at].astype(f32))
            low[at] = (centre * inverse * g1_ref[...].reshape(1, width)).astype(bf16)
        turned[...] = low[...].T

        @pl.loop(0, 3 * width // GROUP)
        def _(n):
            cols = rows_at(n * GROUP, GROUP)
            dense[0:width, cols] = dot(turned[...], gqkv[:, cols]).astype(bf16)

        def rest():
            for r in range(rows // BAND):
                at = slice(r * BAND, (r + 1) * BAND)
                back = dot_nt(gqkv[at], wqkv[...])
                centre, inverse = centred(tok[at].astype(f32))
                unit = centre * inverse
                gains_ref[0:1] += jnp.sum(back * unit, axis=0, keepdims=True)
                slant = back * g1_ref[...].reshape(1, width)
                inner = slant - jnp.mean(slant, axis=-1, keepdims=True)
                inner = inner - unit * jnp.mean(slant * unit, axis=-1, keepdims=True)
                outv[at] = (gh1[at] + inverse * inner).astype(bf16)
            out_three = pltpu.make_async_copy(outv, gtok_out, store.at[0])
            out_three.start()
            for one in y_copies:
                one.wait_recv()
            for r in range(rows // BAND):
                at = slice(r * BAND, (r + 1) * BAND)
                low[at] = (h1[at] + gate[at] * dot(place[at], yr[...])).astype(bf16)
            out_one = pltpu.make_async_copy(low, block_out, store.at[1])
            out_one.start()
            out_one.wait()
            out_three.wait()

        dense_sums(rest)

    def dense_sums(rest):
        chip, core = me // 2, me % 2
        there = flip(me, 1)
        chips = [flip(chip, k) for k in range(half)]
        def send(source, target, ssem, rsem, device):
            return pltpu.make_async_remote_copy(
                src_ref=source, dst_ref=target, send_sem=ssem, recv_sem=rsem, device_id=device,
                device_id_type=MESH,
            )

        started = []

        def go(copy):
            copy.start()
            started.append(copy)
            return copy

        pair = []
        for k in range(half - 1, -1, -1):
            block = chips[k]
            pair.append(
                go(
                    send(
                        dense.at[rows_at(((1 - core) * half + block) * per, per)],
                        other.at[rows_at(block * per, per)],
                        s_pair.at[k], r_pair.at[k], (dp, there),
                    )
                )
            )
        far = {}
        for i, k in enumerate(range(half - 1, -1, -1)):
            at = rows_at(chips[k] * per, per)
            pair[i].wait_recv()
            other[at] = add(dense[rows_at((core * half + chips[k]) * per, per)], other[at])
            if k:
                far[k] = go(
                    send(other.at[at], got.at[k], s_chip.at[k], r_chip.at[k], (dp, chips[k] * 2 + core))
                )
        rest()
        gain_pair = go(send(gains_ref, gains_pair, s_gain.at[0], r_gain.at[0], (dp, there)))
        third()
        gain_pair.wait_recv()
        gains_part[0] = gains_ref[...] + gains_pair[...]
        gain_far = [
            go(
                send(
                    gains_part.at[0], gains_chip.at[k], s_gain.at[k], r_gain.at[k],
                    (dp, chips[k] * 2 + core),
                )
            )
            for k in range(1, half)
        ]
        total = other[rows_at(chip * per, per)].astype(f32)
        for k in range(1, half):
            far[k].wait_recv()
            total = total + got[k].astype(f32)
        share = 3 * width // copies
        thin = width // copies
        for d in range(copies):
            ring[d] = jnp.concatenate(
                [
                    total[:, d * share : (d + 1) * share],
                    total[:, 3 * width + d * thin : 3 * width + (d + 1) * thin],
                ],
                axis=1,
            ).astype(bf16)
        around = [
            go(send(ring.at[rounds[k]], ring_got.at[k], s_ring.at[k], r_ring.at[k], (rounds[k], me)))
            for k in range(1, copies)
        ]
        gains = gains_part[0]
        for k in range(1, half):
            gain_far[k - 1].wait_recv()
            gains = gains + gains_chip[k]
        gains_part[1] = gains
        gain_around = [
            go(
                send(
                    gains_part.at[1], gains_ring.at[k], s_gain.at[half + k], r_gain.at[half + k],
                    (rounds[k], me),
                )
            )
            for k in range(1, copies)
        ]
        summed = ring[dp].astype(f32)
        for k in range(1, copies):
            around[k - 1].wait_recv()
            summed = summed + ring_got[k].astype(f32)
        place = rows_at((core * half + chip) * per, per)
        final[...] = summed.astype(bf16)
        whole[place] = final[...]
        spread = [
            go(send(final, whole.at[place], s_out.at[k], r_out.at[k], (dp, flip(me, k))))
            for k in range(groups - 1, 0, -1)
        ]
        for k in range(1, copies):
            gain_around[k - 1].wait_recv()
            gains = gains + gains_ring[k]
        total_ref[...] = gains
        for one in spread:
            one.wait_recv()
        last = pltpu.make_async_copy(whole, whole_out, store.at[2])
        last.start()
        last.wait()
        for one in started:
            one.wait_send()

    pl.run_scoped(
        dense_part,
        pltpu.VMEM((rows, width), f32), pltpu.VMEM((rows, width), bf16),
        pltpu.VMEM((rows, width), bf16), pltpu.VMEM((rows, width), bf16),
        pltpu.VMEM((rows, width), f32), pltpu.VMEM(probs_hbm.shape, bf16),
        pltpu.VMEM((rows, 3 * width), bf16), pltpu.VMEM((width, 3 * width), bf16),
        pltpu.VMEM((width, width), bf16), pltpu.VMEM((rows, slots), bf16),
        pltpu.VMEM((rows, width), f32), pltpu.VMEM((rows, width), bf16),
        pltpu.VMEM((rows, width), bf16), pltpu.VMEM((rows, width), f32),
        pltpu.VMEM((rows, 3 * width), bf16), pltpu.VMEM((width, rows), bf16),
        pltpu.VMEM((rows, PAIR), f32), pltpu.VMEM((rows, PAIR), f32),
        pltpu.VMEM((rows, width), bf16),
    )
    for one in gv_copies + y_copies:
        one.wait_send()
    if ends:
        for i in range(9):
            if i not in (0, 3, 4):
                relay.landed(i)
            if i > 1:
                relay.sent(i)


def backward(
    groups, cap, copies, ends, per, act, gpre, w_in, w_down, experts, gates, h1, cot, tok, g1, g2, att,
    inv, probs, qkv, w_qkv, w_out, parts,
):
    slots, hidden = act.shape
    rows, width = tok.shape
    wide = 4 * width
    half = groups // 2
    thin = wide // copies
    sems = pltpu.SemaphoreType.DMA
    block = pltpu.VMEM((slots, width), bf16)
    tile = (8, width)
    up = (width // 4, hidden)
    down = (hidden // 4, width)
    land = [up, down, up, down, up, up, down, down, up] if ends else []
    pools = [up, up, down, up] if ends else []
    return pl.pallas_call(
        functools.partial(backward_kernel, groups, cap, copies, ends),
        out_shape=[
            jax.ShapeDtypeStruct((rows, width), bf16), jax.ShapeDtypeStruct((rows, width), bf16),
            jax.ShapeDtypeStruct((groups * per, thin), bf16), jax.ShapeDtypeStruct(tile, f32),
        ]
        + [jax.ShapeDtypeStruct(one, bf16) for one in land],
        in_specs=[ANY] * 4 + [VMEM] * 2 + [ANY] * 3 + [VMEM] * 2 + [ANY] * (6 + len(parts)),
        out_specs=[ANY] * 3 + [VMEM] + [ANY] * len(land),
        scratch_shapes=[
            block, block, block, block,
            pltpu.VMEM((groups * per, wide), bf16), pltpu.VMEM((half * per, wide), bf16),
            pltpu.VMEM((half, per, wide), bf16), pltpu.VMEM((copies, per, thin), bf16),
            pltpu.VMEM((copies, per, thin), bf16), pltpu.VMEM((per, thin), bf16),
            pltpu.VMEM((groups * per, thin), bf16), pltpu.VMEM(tile, f32), pltpu.VMEM(tile, f32),
            pltpu.VMEM((half, *tile), f32), pltpu.VMEM((2, *tile), f32),
            pltpu.VMEM((copies, *tile), f32), sems((9,)), sems((3,)), sems((groups,)),
            sems((groups,)), sems((groups,)), sems((groups,)), sems((half,)), sems((half,)),
            sems((half,)), sems((half,)), sems((copies,)), sems((copies,)), sems((groups,)),
            sems((groups,)), sems((half + copies,)), sems((half + copies,)), sems((9,)), sems((9,)),
            sems((2,)),
        ]
        + [pltpu.VMEM(one, bf16) for one in pools]
        + [pltpu.VMEM(one, bf16) for one in (up, down) if ends],
        compiler_params=pltpu.CompilerParams(
            collective_id=1, has_side_effects=True, vmem_limit_bytes=60 * MIB
        ),
        cost_estimate=pl.CostEstimate(
            flops=200 * 10**9, bytes_accessed=40 * 10**6, transcendentals=0
        ),
        name="backward",
    )(
        act, gpre, w_in, w_down, experts, gates, h1, cot, tok, g1, g2, att, inv, probs, qkv, w_qkv,
        w_out, *parts,
    )


def finish_kernel(*refs):
    (
        up_own, up_in, up_across, up_out, up_outward, down_own, down_in, down_across, down_out,
        down_outward, block, gtok, whole_ref, gains_ref, up_ref, down_ref, qkv_hbm, out_hbm, one_ref,
        two_ref, block_ref, gtok_ref, a, b, c, d, e, f, up, down, qkv_ref, out_ref,
        block_line, gtok_line, load, store,
    ) = refs
    dp = lax.axis_index("dp")
    outer = (dp == 0) | (dp == 3)
    inner = jnp.logical_not(outer)
    hand_in = [
        pltpu.make_async_copy(block, block_line, load.at[6]),
        pltpu.make_async_copy(gtok, gtok_line, load.at[7]),
    ]
    handed = [
        pltpu.make_async_copy(block_line, block_ref, store.at[0]),
        pltpu.make_async_copy(gtok_line, gtok_ref, store.at[1]),
    ]

    def loads(sources, targets):
        return [
            pltpu.make_async_copy(src, dst, load.at[i])
            for i, (src, dst) in enumerate(zip(sources, targets))
        ]

    inside = loads((up_own, up_in, up_across, down_own, down_in, down_across), (a, b, c, d, e, f))
    outside = loads((up_out, up_outward, down_out, down_outward), (a, b, d, e))

    @pl.when(inner)
    def _():
        for one in inside:
            one.start()

    @pl.when(outer)
    def _():
        for one in outside:
            one.start()

    for one in hand_in:
        one.start()
    thin = qkv_ref.shape[0]
    turned = whole_ref[...].astype(f32).T
    qkv_ref[...] = turned[:thin]
    out_ref[...] = turned[thin:]
    handed += [
        pltpu.make_async_copy(qkv_ref, qkv_hbm, store.at[4]),
        pltpu.make_async_copy(out_ref, out_hbm, store.at[5]),
    ]
    for one in hand_in:
        one.wait()
    for one in handed:
        one.start()
    size = one_ref.shape[1]
    for row, target in ((0, one_ref), (1, two_ref)):
        line = jnp.zeros((1, size), f32)
        for plane in range(4):
            part = gains_ref[row : row + 1, plane * size : (plane + 1) * size]
            line = jnp.where(dp == plane, part, line)
        target[...] = line

    def summed(target, terms):
        lines = target.shape[0] // 12

        @pl.loop(0, 12)
        def _(r):
            at = rows_at(r * lines, lines)
            total = terms[0][at].astype(f32)
            for term in terms[1:]:
                total = total + term[at].astype(f32)
            target[at] = total

    up_store = pltpu.make_async_copy(up, up_ref, store.at[2])
    down_store = pltpu.make_async_copy(down, down_ref, store.at[3])

    @pl.when(inner)
    def _():
        for one in inside[:3]:
            one.wait()
        summed(up, (a, b, c))
        up_store.start()
        for one in inside[3:]:
            one.wait()
        summed(down, (d, e, f))

    @pl.when(outer)
    def _():
        for one in outside[:2]:
            one.wait()
        summed(up, (a, b))
        up_store.start()
        for one in outside[2:]:
            one.wait()
        summed(down, (d, e))

    down_store.start()
    for one in handed:
        one.wait()
    up_store.wait()
    down_store.wait()


def finish(ups, downs, block, gtok, whole, gains):
    up, down = ups[0].shape, downs[0].shape
    width = whole.shape[1]
    thin = width // 4
    sems = pltpu.SemaphoreType.DMA
    return pl.pallas_call(
        finish_kernel,
        out_shape=[
            jax.ShapeDtypeStruct(up, f32), jax.ShapeDtypeStruct(down, f32),
            jax.ShapeDtypeStruct((3 * thin, whole.shape[0]), f32),
            jax.ShapeDtypeStruct((thin, whole.shape[0]), f32),
            jax.ShapeDtypeStruct((1, thin), f32), jax.ShapeDtypeStruct((1, thin), f32),
            jax.ShapeDtypeStruct(block.shape, bf16), jax.ShapeDtypeStruct(gtok.shape, bf16),
        ],
        in_specs=[ANY] * 12 + [VMEM] * 2,
        out_specs=[ANY] * 4 + [VMEM] * 2 + [ANY] * 2,
        scratch_shapes=[pltpu.VMEM(up, bf16)] * 3
        + [pltpu.VMEM(down, bf16)] * 3
        + [
            pltpu.VMEM(up, f32), pltpu.VMEM(down, f32), pltpu.VMEM((3 * thin, whole.shape[0]), f32),
            pltpu.VMEM((thin, whole.shape[0]), f32), pltpu.VMEM(block.shape, bf16),
            pltpu.VMEM(gtok.shape, bf16), sems((8,)), sems((6,)),
        ],
        compiler_params=pltpu.CompilerParams(vmem_limit_bytes=60 * MIB),
        name="finish",
    )(*ups, *downs, block, gtok, whole, gains)


def shards(
    tokens, segment_ids, token_expert, gates, ln1_gain, w_qkv, w_out, ln2_gain, expert_in,
    expert_out, cotangent,
):
    rows, width = tokens.shape
    groups, copies = lax.axis_size("expert"), lax.axis_size("dp")
    cap = 2 * rows // groups
    per = -(-width // (16 * groups)) * 16
    w_in, w_down = expert_in[0], expert_out[0]
    experts, gate_row = token_expert.reshape(1, rows), gates.reshape(1, rows)
    ends = copies == 4
    h1, qkv, att, inv, probs, act, gpre, *parts = forward(
        groups, cap, ends, tokens, segment_ids, experts, gate_row, ln1_gain, w_qkv, w_out,
        ln2_gain, w_in, w_down, cotangent,
    )
    if ends:
        up_far, up_near, up_out, up_own, down_far, down_near, down_out, down_own, up_far_in = parts
        parts = [up_far, up_near, up_out, up_own, up_far_in, down_far, down_near, down_out, down_own]
    block_out, grad_tokens, whole, gains, *landed = backward(
        groups, cap, copies, ends, per, act, gpre, w_in, w_down, experts, gate_row, h1, cotangent,
        tokens, ln1_gain, ln2_gain, att, inv, probs, qkv, w_qkv, w_out, parts if ends else [],
    )
    if ends:
        _, down_own_in, up_own_in, _, _, up_across, down_across, down_outward, up_outward = landed
        up_share, down_share, share_qkv, share_out, share_one, share_two, block, gtok = finish(
            (up_own, up_own_in, up_across, up_out, up_outward),
            (down_own, down_own_in, down_across, down_out, down_outward),
            block_out, grad_tokens, whole[:width], gains,
        )
        return (
            block, gtok, share_one[0], share_qkv.T, share_out.T, share_two[0], up_share[None],
            down_share[None],
        )
    up_share, down_share = (
        lax.psum_scatter(one[None], "dp", scatter_dimension=1, tiled=True) for one in parts
    )
    whole = whole[:width].astype(f32)
    share = width // copies
    gains = lax.dynamic_slice_in_dim(gains, lax.axis_index("dp") * share, share, 1)
    return (
        block_out,
        grad_tokens,
        gains[0],
        whole[:, : 3 * share],
        whole[:, 3 * share :],
        gains[1],
        up_share.astype(f32),
        down_share.astype(f32),
    )


def solution(mesh):
    tokens, experts = P(("dp", "expert"), None), P("expert", None, None)
    return jax.shard_map(
        shards,
        mesh=mesh,
        in_specs=(
            tokens, tokens, tokens, P(("dp", "expert")), P(), P(), P(), P(), experts, experts,
            tokens,
        ),
        out_specs=(
            tokens, tokens, P("dp"), P(None, "dp"), P(None, "dp"), P("dp"),
            P("expert", "dp", None), P("expert", "dp", None),
        ),
        check_vma=False,
    )
```

profile of v0, /device:TPU:25, one launch (start us, length us, event | category | flops | bytes accessed | tf_op | source)
XLA Modules:
  0.0 250.0 jit_solution(15144290404494691064)
XLA Ops:
  0.6 84.5 %forward.1 = (f32[512,768]{1,0:T(8,128)}, bf16[512,2304]{1,0:T(8,128)(2,1)}, bf16[512,768]{1,0:T(8,128)(2,1)}, f32[512,768]{1,0:T(8,128)}, bf16[6,1024,384]{2,1,...) custom-call(bf16[512,768]{1,0:T(8,128)(2,1)} %refs_8_.1, ...), custom_call_target="tpu_custom_call" | custom-call | flops 199999995904 | bytes 40000000 | tf_op jit(solution)/shard_map/forward/pallas_call | solution.py:512
  85.2 156.4 %backward.1 = (bf16[512,768]{1,0:T(8,128)(2,1)}, bf16[512,768]{1,0:T(8,128)(2,1)}, bf16[768,768]{1,0:T(8,128)(2,1)}, f32[8,768]{1,0:T(8,128)}, bf16[192,3072]{1,...) custom-call(bf16[1024,3072]{1,0:T(8,128)(2,1)} %get-tuple-element.43, ...), custom_call_target="tpu_custom_call" | custom-call | flops 199999995904 | bytes 40000000 | tf_op jit(solution)/shard_map/backward/pallas_call | solution.py:939
  241.6 8.2 %finish.1 = (f32[192,3072]{1,0:T(8,128)}, f32[768,768]{1,0:T(8,128)}, f32[576,768]{1,0:T(8,128)}, f32[192,768]{1,0:T(8,128)}, f32[1,192]{1,0:T(1,128)}, /*index=...) custom-call(bf16[192,3072]{1,0:T(8,128)(2,1)} %get-tuple-element.42.refs_20_.refs_0_, ...), custom_call_target="tpu_custom_call" | custom-call | tf_op jit(solution)/shard_map/finish/pallas_call | solution.py:1082
where the time goes:
time: 250 us
  Pallas kernels  249 us (100%)
    pallas_call x1, Pallas kernels, backward(): pl.pallas_call(functools.partial(backward_kernel, groups, cap, copies, en...  156 us
    pallas_call x1, Pallas kernels, forward(): pl.pallas_call(functools.partial(forward_kernel, groups, cap, int(ends)),...  84.5 us
    pallas_call x1, Pallas kernels, finish(): pl.pallas_call(finish_kernel, out_shape=[jax.ShapeDtypeStruct(up, f32), j...  8.24 us

commit v1 on v0

--- a/solution.py
+++ b/solution.py
@@ -141,13 +141,8 @@
 
 
 def gelu_pair(x):
-    bell = jnp.exp(-0.5 * x * x)
-    t = 1.0 / (1.0 + (0.3275911 * 0.7071067811865476) * jnp.abs(x))
-    poly = 0.5 * 1.061405429
-    for factor in (-1.453152027, 1.421413741, -0.284496736, 0.254829592):
-        poly = poly * t + 0.5 * factor
-    tail = poly * t * bell
-    phi = jnp.where(x >= 0.0, 1.0 - tail, tail)
+    bell = jnp.exp2((-0.5 * 1.4426950408889634) * (x * x))
+    phi = 0.5 + 0.5 * lax.erf(x * 0.7071067811865476)
     return x * phi, phi + x * (bell * 0.3989422804014327)
 
 
@@ -165,7 +160,7 @@
     up_land = refs[18 + 2 * count : 18 + 2 * count + ends]
     (
         tok, cot, win, wdown, low, h1, place, sent, gy_send, gy_got, v_got, gy_low, spot_own, gy_line,
-        v_line, spot_far, gy_fsend, far_send, gy_far, v_far, act,
+        v_line, spot_far, place_far, gy_fsend, far_send, gy_far, v_far, act,
         gpre, load, store, act_store, gpre_store, gy_ssem, gy_rsem, v_ssem, v_rsem, gy_fssem,
         gy_frsem, v_fssem, v_frsem, line_ssem, line_rsem, rel_s, rel_r,
     ) = refs[18 + 2 * count + ends :]
@@ -216,25 +211,31 @@
         if ends:
             pl.when(condition)(action)
 
-    def placed(line, target):
+    def positions(spot, target):
         @pl.loop(0, slots // GROUP)
         def _(g):
-            at = rows_at(g * GROUP, GROUP)
             here = lax.broadcasted_iota(jnp.int32, (GROUP, rows), 0) + g * GROUP
-            there = jnp.where(here.astype(f32) == spot_far[0:1], 1.0, 0.0).astype(bf16)
-            target[at] = dot(there, line[...]).astype(bf16)
+            there = jnp.where(here.astype(f32) == spot, 1.0, 0.0)
+            target[rows_at(g * GROUP, GROUP)] = there.astype(bf16)
+
+    def placed(where, line, target):
+        @pl.loop(0, width // GROUP)
+        def _(n):
+            cols = rows_at(n * GROUP, GROUP)
+            target[:, cols] = dot(where[...], line[:, cols]).astype(bf16)
 
     def far_gy():
         lines[0].wait_recv()
         lines[1].wait_recv()
-        placed(gy_line, gy_fsend)
+        positions(spot_far[0:1], place_far)
+        placed(place_far, gy_line, gy_fsend)
         for one in gy_fars:
             one.start()
         gy_far[mine] = gy_fsend[mine]
 
     def far_v():
         lines[2].wait_recv()
-        placed(v_line, far_send)
+        placed(place_far, v_line, far_send)
         for one in v_fars:
             one.start()
         v_far[mine] = far_send[mine]
@@ -250,12 +251,7 @@
             one.start()
         spot = slot_row(te_ref[...], groups, cap)
 
-        @pl.loop(0, slots // GROUP)
-        def _(g):
-            here = lax.broadcasted_iota(jnp.int32, (GROUP, rows), 0) + g * GROUP
-            there = jnp.where(here.astype(f32) == spot, 1.0, 0.0)
-            place[rows_at(g * GROUP, GROUP)] = there.astype(bf16)
-
+        positions(spot, place)
         first_loads[0].wait()
         gate = column_of(gate_ref[...])
         gy_low[...] = (gate * cot[...].astype(f32)).astype(bf16)
@@ -267,11 +263,7 @@
                 lines[0].start()
                 lines[1].start()
 
-        @pl.loop(0, slots // GROUP)
-        def _(g):
-            at = rows_at(g * GROUP, GROUP)
-            gy_send[at] = dot(place[at], gy_low[...]).astype(bf16)
-
+        placed(place, gy_low, gy_send)
         for one in gy_copies:
             one.start()
         gy_got[mine] = gy_send[mine]
@@ -339,21 +331,22 @@
             one.start()
         loads[1].wait()
 
+        @pl.loop(0, width // GROUP)
+        def _(n):
+            cols = rows_at(n * GROUP, GROUP)
+            h1[:, cols] = dot(att[...], wout[:, cols])
+
         @pl.loop(0, rows // BAND)
         def _(r):
             at = rows_at(r * BAND, BAND)
-            resid = tok[at].astype(f32) + dot(att[at], wout[...])
+            resid = tok[at].astype(f32) + h1[at]
             h1[at] = resid
             centre, inverse = centred(resid)
             low[at] = (centre * inverse * g2_ref[...].reshape(1, width)).astype(bf16)
 
         when(outer, lambda: lines[2].start())
 
-        @pl.loop(0, slots // GROUP)
-        def _(g):
-            at = rows_at(g * GROUP, GROUP)
-            sent[at] = dot(place[at], low[...]).astype(bf16)
-
+        placed(place, low, sent)
         for one in v_copies:
             one.start()
         v_got[mine] = sent[mine]
@@ -450,11 +443,10 @@
                 at = rows_at(flip(me // many, g) * GROUP, GROUP)
                 for i in range(2):
 
-                    @pl.loop(0, share // CHUNK + share % CHUNK // GROUP)
+                    @pl.loop(0, 2)
                     def _(c):
-                        wide = share // (share // CHUNK + share % CHUNK // GROUP)
-                        cols = pl.ds(pl.multiple_of(shares[i] * share + c * wide, 128), wide)
-                        kept = pl.ds(pl.multiple_of(i * share + c * wide, 128), wide)
+                        cols = pl.ds(pl.multiple_of(shares[i] * share + c * (share // 2), 128), share // 2)
+                        kept = pl.ds(pl.multiple_of(i * share + c * (share // 2), 128), share // 2)
                         act_far[at, kept] = gelu(dot(v_far[at], win[:, cols])).astype(bf16)
 
             for one in gy_fars:
@@ -518,7 +510,7 @@
             lines, lines, pltpu.VMEM(w_in.shape, bf16), pltpu.VMEM(w_down.shape, bf16), lines,
             pltpu.VMEM((rows, width), f32), pltpu.VMEM((slots, rows), bf16), block, block, block,
             block, lines, pltpu.VMEM((8, rows), f32), far_line, far_line, pltpu.VMEM((8, rows), f32),
-            far, far, far, far,
+            pltpu.VMEM((slots, rows) if ends else tiny, bf16), far, far, far, far,
             pltpu.VMEM((slots, hidden), bf16), pltpu.VMEM((slots, hidden), bf16),
             sems((6,)), sems((13,)), sems((slots // GROUP,)), sems((slots // GROUP,)),
         ]
@@ -555,7 +547,7 @@
     rounds = [lax.rem(dp + k, copies) for k in range(copies)]
     half = groups // 2
     per, wide = got.shape[1:]
-    many = GROUP // cap
+    many = CHUNK // cap
     mine = rows_at(me * cap, cap)
 
     def exchange(source, target, ssem, rsem):
@@ -588,9 +580,54 @@
             rel_s, rel_r,
         )
 
+    chip, core = me // 2, me % 2
+    there = flip(me, 1)
+    chips = [flip(chip, k) for k in range(half)]
+    started = []
+    sets = [(0, width), (width, 3 * width // 2), (5 * width // 2, 3 * width // 2)]
+    pair, far = {}, {}
+
+    def send(source, target, ssem, rsem, device):
+        return pltpu.make_async_remote_copy(
+            src_ref=source, dst_ref=target, send_sem=ssem, recv_sem=rsem, device_id=device,
+            device_id_type=MESH,
+        )
+
+    def go(copy):
+        copy.start()
+        started.append(copy)
+        return copy
+
+    def pair_send(i):
+        cols = slice(sets[i][0], sum(sets[i]))
+        pair[i] = go(
+            send(
+                dense.at[rows_at((1 - core) * (half * per), half * per), cols], other.at[:, cols],
+                s_pair.at[i], r_pair.at[i], (dp, there),
+            )
+        )
+
+    def combine(i):
+        cols = slice(sets[i][0], sum(sets[i]))
+        pair[i].wait_recv()
+        for k in range(half - 1, -1, -1):
+            at = rows_at(chips[k] * per, per)
+            own = rows_at((core * half + chips[k]) * per, per)
+            other[at, cols] = add(dense[own, cols], other[at, cols])
+            if k:
+                far[i, k] = go(
+                    send(
+                        other.at[at, cols], got.at[k, :, cols], s_chip.at[3 * k + i],
+                        r_chip.at[3 * k + i], (dp, chips[k] * 2 + core),
+                    )
+                )
+
     def first():
         if ends:
             relay.start(0, 3)
+
+    def between():
+        if ends:
             relay.merged(up_far, up_far_in, pools[0], pools[4], pool_sem)
             relay.start(4)
 
@@ -601,16 +638,21 @@
             relay.landed(0)
             relay.merged(up_near, landed[0], pools[1], pools[4], pool_sem)
             relay.start(5)
+            relay.landed(3)
+            relay.merged(down_out, landed[3], pools[2], pools[5], pool_sem)
+            relay.start(7)
 
     def third():
         if ends:
             relay.sent(1)
-            relay.start(2, 6)
-            relay.landed(3)
-            relay.merged(down_out, landed[3], pools[2], pools[5], pool_sem)
+            relay.start(2)
             relay.landed(4)
             relay.merged(up_out, landed[4], pools[3], pools[4], pool_sem)
-            relay.start(7, 8)
+            relay.start(8)
+
+    def fourth():
+        if ends:
+            relay.start(6)
 
     def experts(act, gpre, win, wdown):
         loads = [
@@ -627,8 +669,8 @@
         first()
         for one in loads[:2]:
             one.wait()
-        for g in range(slots // GROUP - 1, -1, -1):
-            at = rows_at(flip(me // many, g) * GROUP, GROUP)
+        for g in range(slots // CHUNK - 1, -1, -1):
+            at = rows_at(flip(me // many, g) * CHUNK, CHUNK)
 
             @pl.loop(0, width // GROUP)
             def _(n):
@@ -646,6 +688,8 @@
         def _(n):
             cols = rows_at(n * GROUP, GROUP)
             y_send[:, cols] = dot(act[...], wdown[:, cols]).astype(bf16)
+
+        between()
 
     pl.run_scoped(
         experts,
@@ -680,12 +724,17 @@
         for one in y_copies:
             one.start()
         yr[mine] = y_send[mine]
-        second()
         for i in range(2):
             loads[i].wait()
+
+        @pl.loop(0, width // GROUP)
+        def _(n):
+            cols = rows_at(n * GROUP, GROUP)
+            gh1[:, cols] = dot(place[...], gvr[:, cols])
+
         for r in range(rows // BAND):
             at = slice(r * BAND, (r + 1) * BAND)
-            back = dot(place[at], gvr[...])
+            back = gh1[at]
             resid = h1[at]
             centre, inverse = centred(resid)
             unit = centre * inverse
@@ -711,10 +760,16 @@
         @pl.loop(0, width // GROUP)
         def _(n):
             cols = rows_at(n * GROUP, GROUP)
-            dense[0:width, rows_at(3 * width + n * GROUP, GROUP)] = dot(
-                turned[...], low[:, cols]
-            ).astype(bf16)
-
+            dense[0:width, cols] = dot(turned[...], low[:, cols]).astype(bf16)
+
+        pair_send(0)
+        loads[7].wait()
+        for r in range(rows // BAND):
+            at = slice(r * BAND, (r + 1) * BAND)
+            centre, inverse = centred(tok[at].astype(f32))
+            low[at] = (centre * inverse * g1_ref[...].reshape(1, width)).astype(bf16)
+        turned[...] = low[...].T
+        second()
         loads[5].wait()
         loads[6].wait()
         left = lax.broadcasted_iota(jnp.int32, (1, PAIR), 1) < HEAD_DIM
@@ -723,8 +778,7 @@
         def halves(block):
             return jnp.concatenate([jnp.where(left, block, none), jnp.where(left, none, block)], axis=0)
 
-        @pl.loop(0, width // PAIR)
-        def _(h):
+        def attend(h):
             at = rows_at(h * PAIR, PAIR)
             k_at = rows_at(width + h * PAIR, PAIR)
             v_at = rows_at(2 * width + h * PAIR, PAIR)
@@ -752,23 +806,28 @@
                 gvv[seen] += dot_tn(share, grad)
             gqkv[:, k_at] = gk[...].astype(bf16)
             gqkv[:, v_at] = gvv[...].astype(bf16)
-        loads[7].wait()
+        heads = width // PAIR // 2
+        for part in range(2):
+            pl.loop(part * heads, (part + 1) * heads)(attend)
+            for i in range(3):
+                source = i * width + part * heads * PAIR
+                target = width + (3 * part + i) * heads * PAIR
+                dense[0:width, target : target + heads * PAIR] = dot(
+                    turned[...], gqkv[:, source : source + heads * PAIR]
+                ).astype(bf16)
+            pair_send(part + 1)
+            combine(part)
         loads[8].wait()
-        for r in range(rows // BAND):
-            at = slice(r * BAND, (r + 1) * BAND)
-            centre, inverse = centred(tok[at].astype(f32))
-            low[at] = (centre * inverse * g1_ref[...].reshape(1, width)).astype(bf16)
-        turned[...] = low[...].T
-
-        @pl.loop(0, 3 * width // GROUP)
-        def _(n):
-            cols = rows_at(n * GROUP, GROUP)
-            dense[0:width, cols] = dot(turned[...], gqkv[:, cols]).astype(bf16)
 
         def rest():
+            @pl.loop(0, width // GROUP)
+            def _(n):
+                cols = rows_at(n * GROUP, GROUP)
+                inner_sum[:, cols] = dot_nt(gqkv[...], wqkv[cols])
+
             for r in range(rows // BAND):
                 at = slice(r * BAND, (r + 1) * BAND)
-                back = dot_nt(gqkv[at], wqkv[...])
+                back = inner_sum[at]
                 centre, inverse = centred(tok[at].astype(f32))
                 unit = centre * inverse
                 gains_ref[0:1] += jnp.sum(back * unit, axis=0, keepdims=True)
@@ -780,55 +839,22 @@
             out_three.start()
             for one in y_copies:
                 one.wait_recv()
-            for r in range(rows // BAND):
-                at = slice(r * BAND, (r + 1) * BAND)
-                low[at] = (h1[at] + gate[at] * dot(place[at], yr[...])).astype(bf16)
+
+            @pl.loop(0, width // GROUP)
+            def _(n):
+                cols = rows_at(n * GROUP, GROUP)
+                low[:, cols] = (h1[:, cols] + gate * dot(place[...], yr[:, cols])).astype(bf16)
+
             out_one = pltpu.make_async_copy(low, block_out, store.at[1])
             out_one.start()
             out_one.wait()
             out_three.wait()
 
-        dense_sums(rest)
-
-    def dense_sums(rest):
-        chip, core = me // 2, me % 2
-        there = flip(me, 1)
-        chips = [flip(chip, k) for k in range(half)]
-        def send(source, target, ssem, rsem, device):
-            return pltpu.make_async_remote_copy(
-                src_ref=source, dst_ref=target, send_sem=ssem, recv_sem=rsem, device_id=device,
-                device_id_type=MESH,
-            )
-
-        started = []
-
-        def go(copy):
-            copy.start()
-            started.append(copy)
-            return copy
-
-        pair = []
-        for k in range(half - 1, -1, -1):
-            block = chips[k]
-            pair.append(
-                go(
-                    send(
-                        dense.at[rows_at(((1 - core) * half + block) * per, per)],
-                        other.at[rows_at(block * per, per)],
-                        s_pair.at[k], r_pair.at[k], (dp, there),
-                    )
-                )
-            )
-        far = {}
-        for i, k in enumerate(range(half - 1, -1, -1)):
-            at = rows_at(chips[k] * per, per)
-            pair[i].wait_recv()
-            other[at] = add(dense[rows_at((core * half + chips[k]) * per, per)], other[at])
-            if k:
-                far[k] = go(
-                    send(other.at[at], got.at[k], s_chip.at[k], r_chip.at[k], (dp, chips[k] * 2 + core))
-                )
+        combine(2)
         rest()
+        dense_sums()
+
+    def dense_sums():
         gain_pair = go(send(gains_ref, gains_pair, s_gain.at[0], r_gain.at[0], (dp, there)))
         third()
         gain_pair.wait_recv()
@@ -844,22 +870,30 @@
         ]
         total = other[rows_at(chip * per, per)].astype(f32)
         for k in range(1, half):
-            far[k].wait_recv()
+            for i in range(3):
+                far[i, k].wait_recv()
             total = total + got[k].astype(f32)
         share = 3 * width // copies
         thin = width // copies
+        part = width // 2
+        thirds = jnp.concatenate(
+            [
+                total[:, width + (3 * j + i) * part : width + (3 * j + i + 1) * part]
+                for i in range(3)
+                for j in range(2)
+            ],
+            axis=1,
+        )
         for d in range(copies):
             ring[d] = jnp.concatenate(
-                [
-                    total[:, d * share : (d + 1) * share],
-                    total[:, 3 * width + d * thin : 3 * width + (d + 1) * thin],
-                ],
+                [thirds[:, d * share : (d + 1) * share], total[:, d * thin : (d + 1) * thin]],
                 axis=1,
             ).astype(bf16)
         around = [
             go(send(ring.at[rounds[k]], ring_got.at[k], s_ring.at[k], r_ring.at[k], (rounds[k], me)))
             for k in range(1, copies)
         ]
+        fourth()
         gains = gains_part[0]
         for k in range(1, half):
             gain_far[k - 1].wait_recv()
@@ -953,8 +987,8 @@
             pltpu.VMEM((groups * per, thin), bf16), pltpu.VMEM(tile, f32), pltpu.VMEM(tile, f32),
             pltpu.VMEM((half, *tile), f32), pltpu.VMEM((2, *tile), f32),
             pltpu.VMEM((copies, *tile), f32), sems((9,)), sems((3,)), sems((groups,)),
-            sems((groups,)), sems((groups,)), sems((groups,)), sems((half,)), sems((half,)),
-            sems((half,)), sems((half,)), sems((copies,)), sems((copies,)), sems((groups,)),
+            sems((groups,)), sems((groups,)), sems((groups,)), sems((3,)), sems((3,)),
+            sems((3 * half,)), sems((3 * half,)), sems((copies,)), sems((copies,)), sems((groups,)),
             sems((groups,)), sems((half + copies,)), sems((half + copies,)), sems((9,)), sems((9,)),
             sems((2,)),
         ]

time: 250 us -> 227 us (0.908)
  the two profiles are of different devices: /device:TPU:25 before, /device:TPU:8 now
where the time goes in v1:
time: 227 us; the launch traced here: 225 us
  Pallas kernels  224 us (99%)
    pallas_call x1, Pallas kernels, backward(): pl.pallas_call(functools.partial(backward_kernel, groups, cap, copies, en...  129 us
    pallas_call x1, Pallas kernels, forward(): pl.pallas_call(functools.partial(forward_kernel, groups, cap, int(ends)),...  86.2 us
    pallas_call x1, Pallas kernels, finish(): pl.pallas_call(finish_kernel, out_shape=[jax.ShapeDtypeStruct(up, f32), j...  8.91 us

profile of v1, /device:TPU:8, one launch (start us, length us, event | category | flops | bytes accessed | tf_op | source)
XLA Modules:
  0.0 225.0 jit_solution(7459900011098966256)
XLA Ops:
  0.6 86.2 %forward.1 = (f32[512,768]{1,0:T(8,128)}, bf16[512,2304]{1,0:T(8,128)(2,1)}, bf16[512,768]{1,0:T(8,128)(2,1)}, f32[512,768]{1,0:T(8,128)}, bf16[6,1024,384]{2,1,...) custom-call(bf16[512,768]{1,0:T(8,128)(2,1)} %refs_8_.1, ...), custom_call_target="tpu_custom_call" | custom-call | flops 199999995904 | bytes 40000000 | tf_op jit(solution)/shard_map/forward/pallas_call | solution.py:504
  86.9 129.1 %backward.1 = (bf16[512,768]{1,0:T(8,128)(2,1)}, bf16[512,768]{1,0:T(8,128)(2,1)}, bf16[768,768]{1,0:T(8,128)(2,1)}, f32[8,768]{1,0:T(8,128)}, bf16[192,3072]{1,...) custom-call(bf16[1024,3072]{1,0:T(8,128)(2,1)} %get-tuple-element.43, ...), custom_call_target="tpu_custom_call" | custom-call | flops 199999995904 | bytes 40000000 | tf_op jit(solution)/shard_map/backward/pallas_call | solution.py:973
  215.9 8.9 %finish.1 = (f32[192,3072]{1,0:T(8,128)}, f32[768,768]{1,0:T(8,128)}, f32[576,768]{1,0:T(8,128)}, f32[192,768]{1,0:T(8,128)}, f32[1,192]{1,0:T(1,128)}, /*index=...) custom-call(bf16[192,3072]{1,0:T(8,128)(2,1)} %get-tuple-element.42.refs_20_.refs_0_, ...), custom_call_target="tpu_custom_call" | custom-call | tf_op jit(solution)/shard_map/finish/pallas_call | solution.py:1116

commit v2 on v1

--- a/solution.py
+++ b/solution.py
@@ -320,7 +320,6 @@
                 att[here, at] = (jnp.where(left, one, two) * scale).astype(bf16)
 
         pl.loop(0, pairs)(attend)
-        when(inner, far_gy)
         stores = [
             pltpu.make_async_copy(src, dst, store.at[i])
             for i, (src, dst) in enumerate(
@@ -350,6 +349,7 @@
         for one in v_copies:
             one.start()
         v_got[mine] = sent[mine]
+        when(inner, far_gy)
         for one in stores:
             one.wait()
 
@@ -646,6 +646,9 @@
         if ends:
             relay.sent(1)
             relay.start(2)
+
+    def outward():
+        if ends:
             relay.landed(4)
             relay.merged(up_out, landed[4], pools[3], pools[4], pool_sem)
             relay.start(8)
@@ -721,9 +724,6 @@
         gains_ref[...] = jnp.zeros_like(gains_ref)
         for one in gv_copies:
             one.wait_recv()
-        for one in y_copies:
-            one.start()
-        yr[mine] = y_send[mine]
         for i in range(2):
             loads[i].wait()
 
@@ -835,8 +835,9 @@
                 inner = slant - jnp.mean(slant, axis=-1, keepdims=True)
                 inner = inner - unit * jnp.mean(slant * unit, axis=-1, keepdims=True)
                 outv[at] = (gh1[at] + inverse * inner).astype(bf16)
-            out_three = pltpu.make_async_copy(outv, gtok_out, store.at[0])
-            out_three.start()
+            pltpu.make_async_copy(outv, gtok_out, store.at[0]).start()
+
+        def y_part():
             for one in y_copies:
                 one.wait_recv()
 
@@ -848,13 +849,13 @@
             out_one = pltpu.make_async_copy(low, block_out, store.at[1])
             out_one.start()
             out_one.wait()
-            out_three.wait()
+            pltpu.make_async_copy(outv, gtok_out, store.at[0]).wait()
 
         combine(2)
         rest()
-        dense_sums()
-
-    def dense_sums():
+        dense_sums(y_part)
+
+    def dense_sums(y_part):
         gain_pair = go(send(gains_ref, gains_pair, s_gain.at[0], r_gain.at[0], (dp, there)))
         third()
         gain_pair.wait_recv()
@@ -893,7 +894,10 @@
             go(send(ring.at[rounds[k]], ring_got.at[k], s_ring.at[k], r_ring.at[k], (rounds[k], me)))
             for k in range(1, copies)
         ]
-        fourth()
+        outward()
+        for one in y_copies:
+            one.start()
+        yr[mine] = y_send[mine]
         gains = gains_part[0]
         for k in range(1, half):
             gain_far[k - 1].wait_recv()
@@ -912,19 +916,27 @@
         for k in range(1, copies):
             around[k - 1].wait_recv()
             summed = summed + ring_got[k].astype(f32)
+        fourth()
         place = rows_at((core * half + chip) * per, per)
         final[...] = summed.astype(bf16)
         whole[place] = final[...]
         spread = [
-            go(send(final, whole.at[place], s_out.at[k], r_out.at[k], (dp, flip(me, k))))
-            for k in range(groups - 1, 0, -1)
+            go(
+                send(
+                    final, whole.at[place], s_out.at[k], r_out.at[k], (dp, chips[k] * 2 + core)
+                )
+            )
+            for k in range(half - 1, 0, -1)
         ]
+        y_part()
         for k in range(1, copies):
             gain_around[k - 1].wait_recv()
             gains = gains + gains_ring[k]
         total_ref[...] = gains
         for one in spread:
             one.wait_recv()
+        ours = whole.at[rows_at(core * (half * per), half * per)]
+        go(send(ours, ours, s_out.at[0], r_out.at[0], (dp, there))).wait_recv()
         last = pltpu.make_async_copy(whole, whole_out, store.at[2])
         last.start()
         last.wait()

time: 227 us -> 218 us (0.960)
  Pallas kernels: 224 us -> 216 us
    pallas_call x1, Pallas kernels: 129 us -> 124 us  [backward(): pl.pallas_call(functools.partial(backward_kernel, groups, cap, copies, en...]
    pallas_call x1, Pallas kernels: 86.2 us -> 83.5 us  [forward(): pl.pallas_call(functools.partial(forward_kernel, groups, cap, int(ends)),...]
where the time goes in v2:
time: 218 us; the launch traced here: 217 us
  Pallas kernels  216 us (99%)
    pallas_call x1, Pallas kernels, backward(): pl.pallas_call(functools.partial(backward_kernel, groups, cap, copies, en...  124 us
    pallas_call x1, Pallas kernels, forward(): pl.pallas_call(functools.partial(forward_kernel, groups, cap, int(ends)),...  83.5 us
    pallas_call x1, Pallas kernels, finish(): pl.pallas_call(finish_kernel, out_shape=[jax.ShapeDtypeStruct(up, f32), j...  8.91 us

profile of v2, /device:TPU:8, one launch (start us, length us, event | category | flops | bytes accessed | tf_op | source)
XLA Modules:
  0.0 217.3 jit_solution(11497303378761796925)
XLA Ops:
  0.6 83.5 %forward.1 = (f32[512,768]{1,0:T(8,128)}, bf16[512,2304]{1,0:T(8,128)(2,1)}, bf16[512,768]{1,0:T(8,128)(2,1)}, f32[512,768]{1,0:T(8,128)}, bf16[6,1024,384]{2,1,...) custom-call(bf16[512,768]{1,0:T(8,128)(2,1)} %refs_8_.1, ...), custom_call_target="tpu_custom_call" | custom-call | flops 199999995904 | bytes 40000000 | tf_op jit(solution)/shard_map/forward/pallas_call | solution.py:504
  84.2 124.0 %backward.1 = (bf16[512,768]{1,0:T(8,128)(2,1)}, bf16[512,768]{1,0:T(8,128)(2,1)}, bf16[768,768]{1,0:T(8,128)(2,1)}, f32[8,768]{1,0:T(8,128)}, bf16[192,3072]{1,...) custom-call(bf16[1024,3072]{1,0:T(8,128)(2,1)} %get-tuple-element.43, ...), custom_call_target="tpu_custom_call" | custom-call | flops 199999995904 | bytes 40000000 | tf_op jit(solution)/shard_map/backward/pallas_call | solution.py:985
  208.2 8.9 %finish.1 = (f32[192,3072]{1,0:T(8,128)}, f32[768,768]{1,0:T(8,128)}, f32[576,768]{1,0:T(8,128)}, f32[192,768]{1,0:T(8,128)}, f32[1,192]{1,0:T(1,128)}, /*index=...) custom-call(bf16[192,3072]{1,0:T(8,128)(2,1)} %get-tuple-element.42.refs_20_.refs_0_, ...), custom_call_target="tpu_custom_call" | custom-call | tf_op jit(solution)/shard_map/finish/pallas_call | solution.py:1128

commit v3 on v2

--- a/solution.py
+++ b/solution.py
@@ -421,11 +421,13 @@
                 def _(c):
                     cols = pl.ds(pl.multiple_of(shares[i] * share + c * GROUP, GROUP), GROUP)
                     at = pl.ds(pl.multiple_of(i * share + c * GROUP, GROUP), GROUP)
-                    total = dot_tn(act[:, cols], gy_got[...])
                     if shared:
-                        total = total + dot_tn(act_far[:, at], gy_far[...])
+                        total = gdown[at].astype(f32) + dot_tn(act_far[:, at], gy_far[...])
+                    else:
+                        total = dot_tn(act[:, cols], gy_got[...])
                     gdown[at] = total.astype(bf16)
 
+        def leave(kept):
             for i in kept:
                 at = slice(i * share, (i + 1) * share)
                 pltpu.make_async_copy(gdown.at[at], downs[i], store.at[9 + i]).start()
@@ -436,6 +438,7 @@
                 pltpu.make_async_copy(gdown.at[at], downs[i], store.at[9 + i]).wait()
 
         def inside():
+            down([0, 1], False)
             for g in range(slots // GROUP):
                 for k in range(g * many, (g + 1) * many):
                     if k:
@@ -452,11 +455,13 @@
             for one in gy_fars:
                 one.wait_recv()
             down([0, 1], True)
+            leave([0, 1])
             for one in gy_fars + v_fars:
                 one.wait_send()
             taken([0, 1])
 
         down([2, 3] if ends else [0], False)
+        leave([2, 3] if ends else [0])
         if ends:
             pl.when(inner)(inside)
 
@@ -702,7 +707,7 @@
 
     def dense_part(
         h1, cot, tok, att, inv, probs, qkv, wqkv, wout, place, gh1, low, gatt, inner_sum, gqkv,
-        turned, gk, gvv, outv,
+        turned, gk, gvv, outv, lines,
     ):
         loads = [
             pltpu.make_async_copy(src, dst, load.at[i])
@@ -713,8 +718,9 @@
                 )
             )
         ]
-        for one in loads:
-            one.start()
+        loads[7].start()
+        for i in (0, 1, 2, 3, 4, 5, 6, 8):
+            loads[i].start()
         spot = column_of(slot_row(te_ref[...], groups, cap))
         for r in range(rows // BAND):
             at = slice(r * BAND, (r + 1) * BAND)
@@ -722,6 +728,12 @@
             place[at] = jnp.where(here == spot[at], 1.0, 0.0).astype(bf16)
         gate = column_of(gate_ref[...])
         gains_ref[...] = jnp.zeros_like(gains_ref)
+        loads[7].wait()
+        for r in range(rows // BAND):
+            at = slice(r * BAND, (r + 1) * BAND)
+            centre, inverse = centred(tok[at].astype(f32))
+            outv[at] = (centre * inverse * g1_ref[...].reshape(1, width)).astype(bf16)
+        lines[...] = outv[...].T
         for one in gv_copies:
             one.wait_recv()
         for i in range(2):
@@ -763,12 +775,6 @@
             dense[0:width, cols] = dot(turned[...], low[:, cols]).astype(bf16)
 
         pair_send(0)
-        loads[7].wait()
-        for r in range(rows // BAND):
-            at = slice(r * BAND, (r + 1) * BAND)
-            centre, inverse = centred(tok[at].astype(f32))
-            low[at] = (centre * inverse * g1_ref[...].reshape(1, width)).astype(bf16)
-        turned[...] = low[...].T
         second()
         loads[5].wait()
         loads[6].wait()
@@ -813,7 +819,7 @@
                 source = i * width + part * heads * PAIR
                 target = width + (3 * part + i) * heads * PAIR
                 dense[0:width, target : target + heads * PAIR] = dot(
-                    turned[...], gqkv[:, source : source + heads * PAIR]
+                    lines[...], gqkv[:, source : source + heads * PAIR]
                 ).astype(bf16)
             pair_send(part + 1)
             combine(part)
@@ -954,7 +960,7 @@
         pltpu.VMEM((rows, width), bf16), pltpu.VMEM((rows, width), f32),
         pltpu.VMEM((rows, 3 * width), bf16), pltpu.VMEM((width, rows), bf16),
         pltpu.VMEM((rows, PAIR), f32), pltpu.VMEM((rows, PAIR), f32),
-        pltpu.VMEM((rows, width), bf16),
+        pltpu.VMEM((rows, width), bf16), pltpu.VMEM((width, rows), bf16),
     )
     for one in gv_copies + y_copies:
         one.wait_send()
@@ -1059,6 +1065,45 @@
 
     for one in hand_in:
         one.start()
+
+    def summed(target, goal, terms, first):
+        part = target.shape[0] // 3
+        lines = part // 4
+        for piece in range(3):
+
+            @pl.loop(0, 4)
+            def _(r):
+                at = rows_at(piece * part + r * lines, lines)
+                total = terms[0][at].astype(f32)
+                for term in terms[1:]:
+                    total = total + term[at].astype(f32)
+                target[at] = total
+
+            out(target, goal, first, piece).start()
+
+    def out(target, goal, first, piece):
+        part = target.shape[0] // 3
+        at = slice(piece * part, (piece + 1) * part)
+        return pltpu.make_async_copy(target.at[at], goal.at[at], store.at[first + piece])
+
+    @pl.when(inner)
+    def _():
+        for one in inside[:3]:
+            one.wait()
+        summed(up, up_ref, (a, b, c), 6)
+        for one in inside[3:]:
+            one.wait()
+        summed(down, down_ref, (d, e, f), 9)
+
+    @pl.when(outer)
+    def _():
+        for one in outside[:2]:
+            one.wait()
+        summed(up, up_ref, (a, b), 6)
+        for one in outside[2:]:
+            one.wait()
+        summed(down, down_ref, (d, e), 9)
+
     thin = qkv_ref.shape[0]
     turned = whole_ref[...].astype(f32).T
     qkv_ref[...] = turned[:thin]
@@ -1078,46 +1123,11 @@
             part = gains_ref[row : row + 1, plane * size : (plane + 1) * size]
             line = jnp.where(dp == plane, part, line)
         target[...] = line
-
-    def summed(target, terms):
-        lines = target.shape[0] // 12
-
-        @pl.loop(0, 12)
-        def _(r):
-            at = rows_at(r * lines, lines)
-            total = terms[0][at].astype(f32)
-            for term in terms[1:]:
-                total = total + term[at].astype(f32)
-            target[at] = total
-
-    up_store = pltpu.make_async_copy(up, up_ref, store.at[2])
-    down_store = pltpu.make_async_copy(down, down_ref, store.at[3])
-
-    @pl.when(inner)
-    def _():
-        for one in inside[:3]:
-            one.wait()
-        summed(up, (a, b, c))
-        up_store.start()
-        for one in inside[3:]:
-            one.wait()
-        summed(down, (d, e, f))
-
-    @pl.when(outer)
-    def _():
-        for one in outside[:2]:
-            one.wait()
-        summed(up, (a, b))
-        up_store.start()
-        for one in outside[2:]:
-            one.wait()
-        summed(down, (d, e))
-
-    down_store.start()
     for one in handed:
         one.wait()
-    up_store.wait()
-    down_store.wait()
+    for piece in range(3):
+        out(up, up_ref, 6, piece).wait()
+        out(down, down_ref, 9, piece).wait()
 
 
 def finish(ups, downs, block, gtok, whole, gains):
@@ -1141,7 +1151,7 @@
         + [
             pltpu.VMEM(up, f32), pltpu.VMEM(down, f32), pltpu.VMEM((3 * thin, whole.shape[0]), f32),
             pltpu.VMEM((thin, whole.shape[0]), f32), pltpu.VMEM(block.shape, bf16),
-            pltpu.VMEM(gtok.shape, bf16), sems((8,)), sems((6,)),
+            pltpu.VMEM(gtok.shape, bf16), sems((8,)), sems((12,)),
         ],
         compiler_params=pltpu.CompilerParams(vmem_limit_bytes=60 * MIB),
         name="finish",

time: 218 us -> 215 us (0.986)
    pallas_call x1, Pallas kernels: 83.5 us -> 81.2 us  [forward(): pl.pallas_call(functools.partial(forward_kernel, groups, cap, int(ends)),...]
where the time goes in v3:
time: 215 us; the launch traced here: 214 us
  Pallas kernels  214 us (100%)
    pallas_call x1, Pallas kernels, backward(): pl.pallas_call(functools.partial(backward_kernel, groups, cap, copies, en...  124 us
    pallas_call x1, Pallas kernels, forward(): pl.pallas_call(functools.partial(forward_kernel, groups, cap, int(ends)),...  81.2 us
    pallas_call x1, Pallas kernels, finish(): pl.pallas_call(finish_kernel, out_shape=[jax.ShapeDtypeStruct(up, f32), j...  8.33 us

profile of v3, /device:TPU:8, one launch (start us, length us, event | category | flops | bytes accessed | tf_op | source)
XLA Modules:
  0.0 214.4 jit_solution(15882806305147694529)
XLA Ops:
  0.6 81.2 %forward.1 = (f32[512,768]{1,0:T(8,128)}, bf16[512,2304]{1,0:T(8,128)(2,1)}, bf16[512,768]{1,0:T(8,128)(2,1)}, f32[512,768]{1,0:T(8,128)}, bf16[6,1024,384]{2,1,...) custom-call(bf16[512,768]{1,0:T(8,128)(2,1)} %refs_8_.1, ...), custom_call_target="tpu_custom_call" | custom-call | flops 199999995904 | bytes 40000000 | tf_op jit(solution)/shard_map/forward/pallas_call | solution.py:509
  81.8 124.0 %backward.1 = (bf16[512,768]{1,0:T(8,128)(2,1)}, bf16[512,768]{1,0:T(8,128)(2,1)}, bf16[768,768]{1,0:T(8,128)(2,1)}, f32[8,768]{1,0:T(8,128)}, bf16[192,3072]{1,...) custom-call(bf16[1024,3072]{1,0:T(8,128)(2,1)} %get-tuple-element.43, ...), custom_call_target="tpu_custom_call" | custom-call | flops 199999995904 | bytes 40000000 | tf_op jit(solution)/shard_map/backward/pallas_call | solution.py:991
  205.9 8.3 %finish.1 = (f32[192,3072]{1,0:T(8,128)}, f32[768,768]{1,0:T(8,128)}, f32[576,768]{1,0:T(8,128)}, f32[192,768]{1,0:T(8,128)}, f32[1,192]{1,0:T(1,128)}, /*index=...) custom-call(bf16[192,3072]{1,0:T(8,128)(2,1)} %get-tuple-element.42.refs_20_.refs_0_, ...), custom_call_target="tpu_custom_call" | custom-call | tf_op jit(solution)/shard_map/finish/pallas_call | solution.py:1138

commit v4 on v3

--- a/solution.py
+++ b/solution.py
@@ -349,7 +349,6 @@
         for one in v_copies:
             one.start()
         v_got[mine] = sent[mine]
-        when(inner, far_gy)
         for one in stores:
             one.wait()
 
@@ -391,6 +390,8 @@
             for source, target, sem in ((act, act_out, act_store), (gpre, gpre_out, gpre_store)):
                 stores.append(pltpu.make_async_copy(source.at[at], target.at[at], sem.at[g]))
                 stores[-1].start()
+            if g == 0:
+                when(inner, far_gy)
             if g == 1:
                 when(inner, far_v)
 

time: 215 us -> 215 us (level)
  no operation moved by 1% of the time
where the time goes in v4:
time: 215 us; the launch traced here: 214 us
  Pallas kernels  214 us (100%)
    pallas_call x1, Pallas kernels, backward(): pl.pallas_call(functools.partial(backward_kernel, groups, cap, copies, en...  124 us
    pallas_call x1, Pallas kernels, forward(): pl.pallas_call(functools.partial(forward_kernel, groups, cap, int(ends)),...  81.1 us
    pallas_call x1, Pallas kernels, finish(): pl.pallas_call(finish_kernel, out_shape=[jax.ShapeDtypeStruct(up, f32), j...  8.33 us

profile of v4, /device:TPU:8, one launch (start us, length us, event | category | flops | bytes accessed | tf_op | source)
XLA Modules:
  0.0 214.4 jit_solution(16923813580307758522)
XLA Ops:
  0.6 81.1 %forward.1 = (f32[512,768]{1,0:T(8,128)}, bf16[512,2304]{1,0:T(8,128)(2,1)}, bf16[512,768]{1,0:T(8,128)(2,1)}, f32[512,768]{1,0:T(8,128)}, bf16[6,1024,384]{2,1,...) custom-call(bf16[512,768]{1,0:T(8,128)(2,1)} %refs_8_.1, ...), custom_call_target="tpu_custom_call" | custom-call | flops 199999995904 | bytes 40000000 | tf_op jit(solution)/shard_map/forward/pallas_call | solution.py:510
  81.8 124.1 %backward.1 = (bf16[512,768]{1,0:T(8,128)(2,1)}, bf16[512,768]{1,0:T(8,128)(2,1)}, bf16[768,768]{1,0:T(8,128)(2,1)}, f32[8,768]{1,0:T(8,128)}, bf16[192,3072]{1,...) custom-call(bf16[1024,3072]{1,0:T(8,128)(2,1)} %get-tuple-element.43, ...), custom_call_target="tpu_custom_call" | custom-call | flops 199999995904 | bytes 40000000 | tf_op jit(solution)/shard_map/backward/pallas_call | solution.py:992
  205.8 8.3 %finish.1 = (f32[192,3072]{1,0:T(8,128)}, f32[768,768]{1,0:T(8,128)}, f32[576,768]{1,0:T(8,128)}, f32[192,768]{1,0:T(8,128)}, f32[1,192]{1,0:T(1,128)}, /*index=...) custom-call(bf16[192,3072]{1,0:T(8,128)(2,1)} %get-tuple-element.42.refs_20_.refs_0_, ...), custom_call_target="tpu_custom_call" | custom-call | tf_op jit(solution)/shard_map/finish/pallas_call | solution.py:1139
